TPU v7x, 32 devices: a whole 2x2x4 slice. The times are simulated.
32 devices in a mesh: grp: 2 (over y), gx: 4 (over z), gy: 4 (over x, core).
Axes of the slice: x: 2, y: 2, z: 4, core: 2. Of those that a mesh axis runs over, the one named last changes fastest.
Arguments:
- output_gradient: bfloat16 [2048, 10240], P(('grp', 'gx'), 'gy'), parts along dimension 0, may hold values from -6 to 6
- normed_layer_input: bfloat16 [2048, 8192], P(('grp', 'gy'), 'gx'), parts along dimension 0, may hold values from -0.29882812 to 0.29882812
- adapter_hidden: bfloat16 [2048, 64], P(('grp', 'gx')), parts along dimension 0, may hold values from -0.29882812 to 0.29882812
- query_key_value_weight: bfloat16 [8192, 10240], P('gx', 'gy'), may hold values from -0.0625 to 0.0625
- adapter_down_factor: bfloat16 [8, 64, 8192], P('grp', None, 'gx'), parts along dimension 0, may hold values from -0.375 to 0.375
- adapter_up_factor: bfloat16 [8, 64, 10240], P('grp', None, 'gy'), parts along dimension 0, may hold values from -0.0625 to 0.0625
- block_adapter_table: int32 [128, 1], P(('grp', 'gx')), parts along dimension 0, may hold values from 0 to 3; in each aligned block of 16 rows (0 to 15, 16 to 31, ...) at most 8 rows name the same one
- block_live_rows: int32 [128], P(('grp', 'gx')), parts along dimension 0, may hold values from 1 to 16, as said below
Outputs:
- input_gradient: bfloat16 [2048, 8192], P(('grp', 'gy'), 'gx'), parts along dimension 0
- down_gradient: float32 [8, 64, 8192], P(('grp', 'gy'), None, 'gx'), parts along dimension 0
- up_gradient: float32 [8, 64, 10240], P(('grp', 'gx'), None, 'gy'), parts along dimension 0
There are 2 independent parts, one for each index of `grp`. A program takes and returns all parts, laid end to end along the dimension named above; an argument that names none is the same for every part. Nothing has to cross between parts.
Inputs may be any that keep to these rules, and one draw needn't show every extreme that they name: `block_adapter_table`: among the 16 blocks of one index of gx no adapter is named by more than 8 blocks; every adapter names some block. `block_live_rows`: rows of a block past its count are padding; the first block of each index of gx is full.
All inputs are finite; a program needn't handle non-finite values.
Results may differ from a plain program's by a relative error of at most 0.012.
Values may be sent and summed in bfloat16 or wider, within the bound.
A program may use at most 128 MiB of HBM per device.

v0:
```python
import jax
import jax.numpy as jnp
from jax import lax
from jax.sharding import PartitionSpec as P

BLOCK_ROWS = 16


adapter_scale = 2.0


def contract_over_rows(left_side, right_side):
    return lax.dot_general(
        left_side, right_side, (((0,), (0,)), ((), ())), preferred_element_type=jnp.float32
    )


def contract_last(left_side, right_side):
    return lax.dot_general(
        left_side, right_side, (((1,), (1,)), ((), ())), preferred_element_type=jnp.float32
    )


def expand_rows(per_block, block_size):
    return jnp.broadcast_to(per_block[:, None], (per_block.shape[0], block_size)).reshape(-1)


def per_device(
    output_gradient,
    normed_layer_input,
    adapter_hidden,
    query_key_value_weight,
    adapter_down_factor,
    adapter_up_factor,
    block_adapter_table,
    block_live_rows,
):
    tok_local = output_gradient.shape[0]
    block_size = BLOCK_ROWS
    blocks_local = tok_local // block_size
    adapter_rank_width = adapter_up_factor.shape[1]
    width_out = output_gradient.shape[1]
    row_me = lax.axis_index("gx")
    col_me = lax.axis_index("gy")
    offsets = jnp.arange(block_size, dtype=jnp.int32)
    local_adapters = block_adapter_table[:, 0]
    local_live_rows = (offsets[None, :] < block_live_rows[:, None]).reshape(tok_local, 1)
    grad_blocks = output_gradient.reshape(blocks_local, block_size, width_out)
    selected_up = jnp.take(adapter_up_factor, local_adapters, axis=0)
    partial_proj = jnp.einsum(
        "brq,bkq->brk", grad_blocks, selected_up, preferred_element_type=jnp.float32
    ).reshape(tok_local, adapter_rank_width)
    projected_complete = lax.psum(partial_proj.astype(jnp.bfloat16), "gy").astype(jnp.float32)
    adapter_middle = jnp.where(local_live_rows, projected_complete, 0.0).astype(jnp.bfloat16)
    collected_output, gathered_ads, gathered_rows = (
        lax.all_gather(output_gradient, "gx", axis=0, tiled=True),
        lax.all_gather(block_adapter_table, "gx", axis=0, tiled=True),
        lax.all_gather(block_live_rows, "gx", axis=0, tiled=True),
    )
    every_middle = lax.all_gather(adapter_middle, "gx", axis=0, tiled=True)
    every_hidden = lax.all_gather(adapter_hidden, "gx", axis=0, tiled=True)
    frozen_input_gradient = lax.psum_scatter(
        contract_last(collected_output, query_key_value_weight).astype(jnp.bfloat16),
        "gy",
        scatter_dimension=0,
        tiled=True,
    ).astype(jnp.float32)
    all_ads = gathered_ads[:, 0].astype(jnp.int32)
    slot_rows = expand_rows(all_ads, block_size)
    live_all = (offsets[None, :] < gathered_rows[:, None]).reshape(-1, 1)
    mine_adapters = lax.dynamic_slice_in_dim(all_ads, col_me * blocks_local, blocks_local, 0)
    mid_mine = lax.dynamic_slice_in_dim(every_middle, col_me * tok_local, tok_local, 0)
    selected_down = jnp.take(adapter_down_factor, mine_adapters, axis=0)
    adapter_term = jnp.einsum(
        "brk,bki->bri",
        mid_mine.reshape(blocks_local, block_size, adapter_rank_width),
        selected_down,
        preferred_element_type=jnp.float32,
    ).reshape(tok_local, -1)
    input_gradient = (frozen_input_gradient + adapter_scale * adapter_term).astype(jnp.bfloat16)
    every_input = lax.all_gather(normed_layer_input, "gy", axis=0, tiled=True)
    middle_mine = jnp.where((slot_rows == col_me)[:, None], every_middle, 0.0)
    down_gradient = (adapter_scale * contract_over_rows(middle_mine, every_input))[None]
    hidden_valid_rows = jnp.where(live_all, every_hidden, 0.0)
    hidden_mine = jnp.where((slot_rows == row_me)[:, None], hidden_valid_rows, 0.0)
    up_gradient = (adapter_scale * contract_over_rows(hidden_mine, collected_output))[None]
    return (input_gradient, down_gradient, up_gradient)


def solution(mesh):
    placed = (
        P(("grp", "gx"), "gy"),
        P(("grp", "gy"), "gx"),
        P(("grp", "gx"), None),
        P("gx", "gy"),
        P("grp", None, "gx"),
        P("grp", None, "gy"),
        P(("grp", "gx"), None),
        P(("grp", "gx")),
    )
    return jax.shard_map(
        per_device,
        mesh=mesh,
        in_specs=placed,
        out_specs=(
            P(("grp", "gy"), "gx"),
            P(("grp", "gy"), None, "gx"),
            P(("grp", "gx"), None, "gy"),
        ),
        check_vma=False,
    )
```

profile of v0, /device:TPU:0, one launch (start us, length us, event | category | flops | bytes accessed | tf_op | source)
XLA Modules:
  0.0 207.9 jit_solution(11102472524276213815)
XLA Ops:
  7.2 0.7 all-gather.3.cloned.1.call-update
  8.0 0.7 all-gather.5.cloned.1.call-update
  8.7 101.7 %all-gather.3.cloned.1.call-done = bf16[1024,2560]{1,0:T(8,128)(2,1)} async-done(((bf16[256,2560]{1,0:T(8,128)(2,1)}), bf16[1024,2560]{1,0:T(8,128)(2,1)}) %all-gather.3.cloned.1.call-update) | async-done | bytes 5242896 | tf_op jit(solution)/shard_map/all_gather | solution.py:56
  110.4 16.6 %convolution_convert_fusion = bf16[1024,2048]{1,0:T(8,128)(2,1)} fusion(bf16[1024,2560]{1,0:T(8,128)(2,1)} %all-gather.3.cloned.1.call-done, bf16[2048,2560]{1,0:T(8,128)(2,1)} %param.11), kind=kOutput, calls=%fused_computation.8 | convolution fusion | flops 10739515392 | bytes 19922944 | tf_op jit(solution)/shard_map/dot_general | solution.py:19
  127.0 0.6 copy-done.5
  127.7 3.2 %gather_fusion = bf16[16,64,2560]{2,1,0:T(8,128)(2,1)} fusion(bf16[4,64,2560]{2,1,0:T(8,128)(2,1)S(1)} %copy-done, s32[1024]{0:T(1024)S(1)} %pad_clamp_fusion.1), kind=kCustom, calls=%fused_computation | custom fusion | bytes 10485824 | tf_op jit(solution)/shard_map/jit(_take)/gather | solution.py:49
  130.9 4.5 %fusion.14 = bf16[16,64,16]{1,2,0:T(8,128)(2,1)S(1)} fusion(bf16[16,16,2560]{2,1,0:T(8,128)(2,1)} %bitcast.36, bf16[16,64,2560]{2,1,0:T(8,128)(2,1)} %gather_fusion, pred[16]{0:T(512)(128)(4,1)S(1)} %and_bitcast_fusion.1), kind=kOutput, calls=%fused_computation.18 | convolution fusion | flops 86523904 | bytes 6586384 | tf_op jit(solution)/shard_map/brq,bkq->brk/dot_general | solution.py:50
  135.5 0.1 copy.13
  135.7 0.1 lt.61
  135.8 11.9 %psum.7 = bf16[256,64]{0,1:T(8,128)(2,1)S(1)} all-reduce(bf16[256,64]{0,1:T(8,128)(2,1)S(1)} %copy.13), channel_id=1, replica_groups=mesh['grp'=2,'gx'=4,'gy'=4] {'gy'}, use_global_device_ids=true, to_apply=%region_1.2 | all-reduce | flops 16384 | bytes 65536 | tf_op jit(solution)/shard_map/psum | solution.py:53
  147.7 13.3 %all_gather.19 = bf16[1024,64]{0,1:T(8,128)(2,1)S(1)} all-gather(bf16[256,64]{0,1:T(8,128)(2,1)S(1)} %select_convert_fusion), channel_id=1, replica_groups=mesh['grp'=2,'gx'=4,'gy'=4] {'gx'}, dimensions={0}, use_global_device_ids=true | all-gather | bytes 163840 | tf_op jit(solution)/shard_map/all_gather | solution.py:60
  161.0 0.7 copy.14
  161.8 0.6 dynamic-slice.1
  163.0 0.2 dynamic-update-slice.1
  163.4 6.5 %all-reduce.2 = (s32[64]{0:T(128)S(1)}, s32[64]{0:T(128)S(1)}) all-reduce(s32[64]{0:T(128)S(1)} %bitcast_dynamic-update-slice_fusion, s32[64]{0:T(128)S(1)} %dynamic-update-slice.1), channel_id=1, replica_groups=mesh['grp'=2,'gx'=4,'gy'=4] {'gx'}, use_global_device_ids=true, to_apply=%add | all-reduce | flops 128 | bytes 1024
  169.9 0.1 eq.41
  170.1 0.1 lt.69
  170.2 0.1 eq.37
  170.5 2.8 %gather_fusion.1 = bf16[16,64,2048]{2,1,0:T(8,128)(2,1)} fusion(bf16[4,64,2048]{2,1,0:T(8,128)(2,1)S(1)} %copy-done.1, s32[1024]{0:T(1024)S(1)} %pad_clamp_fusion), kind=kCustom, calls=%fused_computation.1 | custom fusion | bytes 8388672 | tf_op jit(solution)/shard_map/jit(_take)/gather | solution.py:73
  173.3 14.1 %all_gather.23 = bf16[1024,64]{0,1:T(8,128)(2,1)} all-gather(bf16[256,64]{0,1:T(8,128)(2,1)S(1)} %copy-done.3), channel_id=1, replica_groups=mesh['grp'=2,'gx'=4,'gy'=4] {'gx'}, dimensions={0}, use_global_device_ids=true | all-gather | bytes 163840 | tf_op jit(solution)/shard_map/all_gather | solution.py:61
  187.4 3.0 %fusion.8 = f32[16,16,2048]{2,1,0:T(8,128)S(1)} fusion(bf16[16,16,64]{2,1,0:T(8,128)(2,1)} %bitcast.37, bf16[16,64,2048]{2,1,0:T(8,128)(2,1)} %gather_fusion.1, pred[16]{0:T(512)(128)(4,1)S(1)} %and_bitcast_fusion), kind=kOutput, calls=%fused_computation.12 | convolution fusion | flops 69730304 | bytes 6324240 | tf_op jit(solution)/shard_map/brk,bki->bri/dot_general | solution.py:74
  190.5 3.9 %fusion.11 = f32[1,64,2048]{2,1,0:T(8,128)} fusion(bf16[1024,2048]{1,0:T(8,128)(2,1)} %all-gather.5.cloned.1.call-done, bf16[1024,64]{0,1:T(8,128)(2,1)S(1)} %all_gather.19, pred[1024]{0:T(1024)(128)(4,1)S(1)} %eq.37), kind=kOutput, calls=%fused_computation.14 | convolution fusion | flops 268632064 | bytes 4850688 | tf_op jit(solution)/shard_map/dot_general | solution.py:13
  194.4 4.4 %fusion.6 = f32[1,64,2560]{2,1,0:T(8,128)} fusion(bf16[1024,2560]{1,0:T(8,128)(2,1)} %all-gather.3.cloned.1.call-done, bf16[1024,64]{0,1:T(8,128)(2,1)S(1)} %copy-done.2, pred[1024]{0:T(1024)(128)(4,1)S(1)} %lt.69, pred[1024]{0:T(1024)(128)(4,1)S(1)} %eq.41), kind=kOutput, calls=%fused_computation.10 | convolution fusion | flops 335839232 | bytes 6031360 | tf_op jit(solution)/shard_map/dot_general | solution.py:13
  198.7 2.6 %fusion.12 = bf16[256,2048]{1,0:T(8,128)(2,1)} fusion(f32[16,16,2048]{2,1,0:T(8,128)S(1)} %fusion.8, bf16[256,2048]{1,0:T(8,128)(2,1)} %reduce-scatter.2.cloned.1.call-done), kind=kLoop, calls=%fused_computation.16 | loop fusion | flops 1572864 | bytes 4194304 | tf_op jit(solution)/shard_map/convert_element_type | solution.py:80
  (35 shorter events, 0.8 us)
Async XLA Ops:
  7.2 120.5 %copy-start = (bf16[4,64,2560]{2,1,0:T(8,128)(2,1)S(1)}, bf16[4,64,2560]{2,1,0:T(8,128)(2,1)}, u32[]{:S(2)}) copy-start(bf16[4,64,2560]{2,1,0:T(8,128)(2,1)} %param.13) | copy-start | bytes 3932164
  7.2 103.2 %all-gather.3.cloned.1.call-start = ((), (), s32[]{:S(2)}) async-start(), calls=%async_computation.1 | async-start | bytes 6553600 | tf_op jit(solution)/shard_map/all_gather | solution.py:56
  7.9 182.5 %all-gather.5.cloned.1.call-start = ((), (), s32[]{:S(2)}) async-start(), calls=%async_computation.3 | async-start | bytes 5242880 | tf_op jit(solution)/shard_map/all_gather | solution.py:81
  8.7 190.1 %reduce-scatter.2.cloned.1.call-start = ((), (), s32[]{:S(2)}) async-start(), calls=%async_computation.2 | async-start | bytes 5242880 | tf_op jit(solution)/shard_map/reduce_scatter | solution.py:62
  127.0 0.7 copy-start.5
  130.9 4.7 %copy-start.4 = (s32[16]{0:T(128)S(1)}, s32[16]{0:T(128)}, u32[]{:S(2)}) copy-start(s32[16]{0:T(128)} %param.15) | copy-start | bytes 196
  130.9 30.9 %copy-start.6 = (u32[32]{0:T(128)S(1)}, u32[32]{0:T(128)}, u32[]{:S(2)}) copy-start(u32[32]{0:T(128)} %constant.55) | copy-start | bytes 388
  130.9 39.5 %copy-start.1 = (bf16[4,64,2048]{2,1,0:T(8,128)(2,1)S(1)}, bf16[4,64,2048]{2,1,0:T(8,128)(2,1)}, u32[]{:S(2)}) copy-start(bf16[4,64,2048]{2,1,0:T(8,128)(2,1)} %param.12) | copy-start | bytes 3145732
  170.4 2.8 %copy-start.3 = (bf16[256,64]{0,1:T(8,128)(2,1)S(1)}, bf16[256,64]{0,1:T(8,128)(2,1)}, u32[]{:S(2)}) copy-start(bf16[256,64]{0,1:T(8,128)(2,1)} %param.10) | copy-start | bytes 98308
  190.4 3.9 %copy-start.2 = (bf16[1024,64]{0,1:T(8,128)(2,1)S(1)}, bf16[1024,64]{0,1:T(8,128)(2,1)}, u32[]{:S(2)}) copy-start(bf16[1024,64]{0,1:T(8,128)(2,1)} %all_gather.23) | copy-start | bytes 393220
Sparse Core Ops, SparseCore 0:
  9.6 100.7 all-gather.2
  111.9 33.1 all-gather.4
  147.6 44.7 reduce-scatter.1
where the time goes:
time: 208 us
  waiting for transfers between devices  103 us (50%)
  blocking collectives  45.8 us (22%)
  matrix products  32.4 us (16%)
  between operations  14.5 us (7%)
  local copies, waits for them, and re-layouts  9 us (4%)
  other arithmetic  2.99 us (1%)
    all_gather x1, waiting for transfers between devices, per_device(): lax.all_gather(output_gradient, 'gx', axis=0, tiled=True)  102 us
    dot_general x1, matrix products, contract_last(): lax.dot_general(left_side, right_side, (((1,), (1,)), ((), ())), preferre...  16.6 us
    all_gather x1, blocking collectives, per_device(): every_hidden = lax.all_gather(adapter_hidden, 'gx', axis=0, tiled=True)  14.1 us
    all_gather x1, blocking collectives, per_device(): every_middle = lax.all_gather(adapter_middle, 'gx', axis=0, tiled=True)  13.3 us
    psum x1, blocking collectives, per_device(): lax.psum(partial_proj.astype(jnp.bfloat16), 'gy').astype(jnp.float32)  11.9 us
    dot_general x2, matrix products, contract_over_rows(): lax.dot_general(left_side, right_side, (((0,), (0,)), ((), ())), preferre...  8.26 us
    unnamed x1, blocking collectives  6.46 us
    dot_general x1, matrix products, per_device(): jnp.einsum('brq,bkq->brk', grad_blocks, selected_up, preferred_element_ty...  4.54 us
  transfers between devices with their start and end apart: 3, of which 1 were waited for; matrix products, arithmetic and copies ran while one was open for 20% of the time, Pallas kernels for 0%

commit v1 on v0

v1 whole, which is shorter than its diff:
```python
import functools

import jax
import jax.numpy as jnp
from jax import lax
from jax.experimental import pallas as pl
from jax.experimental.pallas import tpu as pltpu
from jax.sharding import PartitionSpec as P

BLOCK_ROWS = 16
CHUNK = 64
ADAPTER_SCALE = 2.0
MESH = pl.DeviceIdType.MESH
F32 = jnp.float32
BF16 = jnp.bfloat16


def nt(a, b):
    return lax.dot_general(a, b, (((1,), (1,)), ((), ())), preferred_element_type=F32)


def tn(a, b):
    return lax.dot_general(a, b, (((0,), (0,)), ((), ())), preferred_element_type=F32)


def nn(a, b):
    return lax.dot_general(a, b, (((1,), (0,)), ((), ())), preferred_element_type=F32)


def tile_of(width, most):
    tile = most
    while width % tile:
        tile -= 128
    return tile


def kernel(
    n,
    dy_hbm, x_hbm, hid_ref, w_hbm, down_hbm, up_hbm, ads_ref, live_ref,
    out_ref, dgrad_ref, ugrad_ref,
    dy_all, w, x, down, up, part, part_in, adapter_term,
    hid_out, hid_in, proj_out, proj_in, mid, spread, dpart, dpart_in,
    load_sem, own_sem, z_send, z_recv, rs_send, rs_recv,
    hid_send, hid_recv, proj_send, proj_recv, mid_send, mid_recv, d_send, d_recv,
):
    z = lax.axis_index("gx")
    c_me = lax.axis_index("gy")
    tok, q = dy_hbm.shape
    width = w_hbm.shape[0]
    rank = hid_ref.shape[1]
    nc = tok // CHUNK
    tile_i = tile_of(width, 512)
    tile_q = tile_of(q, 640)

    def rows_of(b, c):
        return pl.ds(pl.multiple_of(b * tok + c * CHUNK, CHUNK), CHUNK)

    def chunk_rows(c):
        return pl.ds(pl.multiple_of(c * CHUNK, CHUNK), CHUNK)

    def own_copy(c):
        return pltpu.make_async_copy(
            dy_hbm.at[chunk_rows(c)], dy_all.at[rows_of(z, c)], own_sem.at[c]
        )

    def z_copy(direction, to, b, c):
        return pltpu.make_async_remote_copy(
            src_ref=dy_all.at[rows_of(b, c)],
            dst_ref=dy_all.at[rows_of(b, c)],
            send_sem=z_send.at[direction, b, c],
            recv_sem=z_recv.at[b, c],
            device_id={"gx": to},
            device_id_type=MESH,
        )

    def rs_copy(src, to, c):
        return pltpu.make_async_remote_copy(
            src_ref=part.at[rows_of(to, c)],
            dst_ref=part_in.at[src, chunk_rows(c)],
            send_sem=rs_send.at[to, c],
            recv_sem=rs_recv.at[src, c],
            device_id={"gy": to},
            device_id_type=MESH,
        )

    def hid_copy(src, to):
        return pltpu.make_async_remote_copy(
            src_ref=hid_out.at[to],
            dst_ref=hid_in.at[src],
            send_sem=hid_send.at[to],
            recv_sem=hid_recv.at[src],
            device_id={"gx": to},
            device_id_type=MESH,
        )

    def proj_copy(src, to):
        return pltpu.make_async_remote_copy(
            src_ref=proj_out,
            dst_ref=proj_in.at[src],
            send_sem=proj_send,
            recv_sem=proj_recv.at[src],
            device_id={"gy": to},
            device_id_type=MESH,
        )

    def mid_copy(to):
        return pltpu.make_async_remote_copy(
            src_ref=mid,
            dst_ref=mid,
            send_sem=mid_send.at[to],
            recv_sem=mid_recv,
            device_id={"gx": to},
            device_id_type=MESH,
        )

    def d_copy(src, to):
        return pltpu.make_async_remote_copy(
            src_ref=dpart.at[to],
            dst_ref=dpart_in.at[src],
            send_sem=d_send.at[to],
            recv_sem=d_recv.at[src],
            device_id={"gy": to},
            device_id_type=MESH,
        )

    loads = [
        pltpu.make_async_copy(up_hbm, up, load_sem.at[0]),
        pltpu.make_async_copy(w_hbm, w, load_sem.at[1]),
        pltpu.make_async_copy(x_hbm, x, load_sem.at[2]),
        pltpu.make_async_copy(down_hbm, down, load_sem.at[3]),
    ]
    for c in range(nc):
        own_copy(c).start()
    for copy in loads:
        copy.start()

    barrier = pltpu.get_barrier_semaphore()
    for step in range(1, n):
        pl.semaphore_signal(
            barrier, inc=1, device_id={"gx": lax.rem(z + step, n)}, device_id_type=MESH
        )
        pl.semaphore_signal(
            barrier, inc=1, device_id={"gy": lax.rem(c_me + step, n)}, device_id_type=MESH
        )
    pl.semaphore_wait(barrier, 2 * (n - 1))

    for c in range(nc):
        own_copy(c).wait()

        @pl.when(z > 0)
        def _():
            z_copy(1, z - 1, z, c).start()

        @pl.when(z < n - 1)
        def _():
            z_copy(0, z + 1, z, c).start()

    block_of = lax.broadcasted_iota(jnp.int32, (1, tok), 1) // BLOCK_ROWS
    offset = lax.broadcasted_iota(jnp.int32, (1, tok), 1) % BLOCK_ROWS
    ad_row = jnp.zeros((1, tok), jnp.int32)
    live_row = jnp.zeros((1, tok), jnp.int32)
    for b in range(tok // BLOCK_ROWS):
        ad_row = jnp.where(block_of == b, ads_ref[b, 0], ad_row)
        live_row = jnp.where(block_of == b, live_ref[b], live_row)
    is_live = offset < live_row

    loads[0].wait()
    own = dy_all[pl.ds(pl.multiple_of(z * tok, tok), tok), :]
    proj = jnp.zeros((rank, tok), F32)
    for s in range(n):
        proj = proj + jnp.where(ad_row == s, nt(up[s * rank:(s + 1) * rank, :], own), 0.0)
    proj_out[...] = proj.astype(BF16)

    @pl.when(c_me != z)
    def _():
        proj_copy(c_me, z).start()

    hid_t = jnp.transpose(hid_ref[...].astype(F32))
    for s in range(n):
        hid_out[s] = jnp.where((ad_row == s) & is_live, hid_t, 0.0).astype(BF16)

        @pl.when(z != s)
        def _():
            hid_copy(z, s).start()

    loads[1].wait()

    def spread_middle():
        @pl.when(c_me == z)
        def _():
            total = proj_out[...].astype(F32)
            for step in range(1, n):
                src = lax.rem(c_me + step, n)
                proj_copy(src, lax.rem(c_me + 1, n)).wait_recv()
                total = total + proj_in[src].astype(F32)
            mid[pl.ds(0, rank), :] = jnp.where(is_live, total, 0.0).astype(BF16)
            mid[pl.ds(rank, 16), :] = jnp.broadcast_to(ad_row.astype(F32), (16, tok)).astype(BF16)
            for step in range(1, n):
                mid_copy(lax.rem(z + step, n)).start()

    def adapter_work():
        @pl.when(c_me != z)
        def _():
            mid_copy(lax.rem(z + 1, n)).wait_recv()

        loads[2].wait()
        loads[3].wait()
        rows_ad = mid[rank:rank + 16, :].astype(F32)[0:1]
        values = mid[0:rank, :].astype(F32)
        for s in range(n):
            spread[s * rank:(s + 1) * rank, :] = jnp.where(rows_ad == float(s), values, 0.0).astype(BF16)

        def column(j, carry):
            cols = pl.ds(pl.multiple_of(j * tile_i, tile_i), tile_i)
            adapter_term[:, cols] = ADAPTER_SCALE * tn(spread[...], down[:, cols])
            grads = nn(spread[...], x[:, cols]).astype(BF16)
            for s in range(n):
                dpart[s, :, cols] = grads[s * rank:(s + 1) * rank]
            return carry

        lax.fori_loop(0, width // tile_i, column, 0)
        for step in range(1, n):
            d_copy(c_me, lax.rem(c_me + step, n)).start()

    def body(i, carry):
        @pl.when(i == 2 * nc)
        def _():
            spread_middle()

        @pl.when(i == 4 * nc)
        def _():
            adapter_work()

        d = i // (2 * nc)
        c = (i % (2 * nc)) // 2
        side = i % 2
        b = z + d * (2 * side - 1)

        @pl.when((b >= 0) & (b < n) & ((d > 0) | (side == 0)))
        def _():
            @pl.when(d > 0)
            def _():
                z_copy(side, lax.rem(z + 1, n), b, c).wait_recv()

                @pl.when((side == 0) & (z < n - 1))
                def _():
                    z_copy(0, z + 1, b, c).start()

                @pl.when((side == 1) & (z > 0))
                def _():
                    z_copy(1, z - 1, b, c).start()

            rows = rows_of(b, c)

            def column(j, carry):
                cols = pl.ds(pl.multiple_of(j * tile_i, tile_i), tile_i)
                part[rows, cols] = nt(dy_all[rows, :], w[cols, :]).astype(BF16)
                return carry

            lax.fori_loop(0, width // tile_i, column, 0)

            @pl.when(b != c_me)
            def _():
                rs_copy(c_me, b, c).start()

        return carry

    lax.fori_loop(0, 2 * nc * n, body, 0)

    for step in range(1, n):
        hid_copy(lax.rem(z + step, n), lax.rem(z + 1, n)).wait_recv()
    hid_in[z] = hid_out[z]

    def up_column(j, carry):
        cols = pl.ds(pl.multiple_of(j * tile_q, tile_q), tile_q)
        total = jnp.zeros((rank, tile_q), F32)
        for b in range(n):
            total = total + nn(hid_in[b], dy_all[b * tok:(b + 1) * tok, cols])
        ugrad_ref[:, cols] = ADAPTER_SCALE * total
        return carry

    lax.fori_loop(0, q // tile_q, up_column, 0)

    total = dpart[c_me].astype(F32)
    for step in range(1, n):
        src = lax.rem(c_me + step, n)
        d_copy(src, lax.rem(c_me + 1, n)).wait_recv()
        total = total + dpart_in[src].astype(F32)
    dgrad_ref[...] = ADAPTER_SCALE * total

    def finish(c, carry):
        rows = chunk_rows(c)
        total = adapter_term[rows, :] + part[rows_of(c_me, c), :].astype(F32)
        for step in range(1, n):
            src = lax.rem(c_me + step, n)
            rs_copy(src, lax.rem(c_me + 1, n), c).wait_recv()
            total = total + part_in[src, rows, :].astype(F32)
        out_ref[rows, :] = total.astype(BF16)
        return carry

    lax.fori_loop(0, nc, finish, 0)

    def drain(i, carry):
        b = i // nc
        c = i % nc

        @pl.when((b <= z) & (z < n - 1))
        def _():
            z_copy(0, z + 1, b, c).wait_send()

        @pl.when((b >= z) & (z > 0))
        def _():
            z_copy(1, z - 1, b, c).wait_send()

        @pl.when(b != c_me)
        def _():
            rs_copy(c_me, b, c).wait_send()

        return carry

    lax.fori_loop(0, n * nc, drain, 0)
    for step in range(1, n):
        hid_copy(z, lax.rem(z + step, n)).wait_send()
        d_copy(c_me, lax.rem(c_me + step, n)).wait_send()

        @pl.when(c_me == z)
        def _():
            mid_copy(lax.rem(z + step, n)).wait_send()

    @pl.when(c_me != z)
    def _():
        proj_copy(c_me, z).wait_send()


def per_device(n, dy, x, hidden, w, down, up, ads, live):
    tok, q = dy.shape
    width = w.shape[0]
    count, rank = down.shape[0], down.shape[1]
    nc = tok // CHUNK
    any_space = pl.BlockSpec(memory_space=pl.ANY)
    in_vmem = pl.BlockSpec(memory_space=pltpu.VMEM)
    in_smem = pl.BlockSpec(memory_space=pltpu.SMEM)
    dma = pltpu.SemaphoreType.DMA
    out, dgrad, ugrad = pl.pallas_call(
        functools.partial(kernel, n),
        out_shape=(
            jax.ShapeDtypeStruct((tok, width), BF16),
            jax.ShapeDtypeStruct((rank, width), F32),
            jax.ShapeDtypeStruct((rank, q), F32),
        ),
        in_specs=[any_space, any_space, in_vmem, any_space, any_space, any_space, in_smem, in_smem],
        out_specs=(in_vmem, in_vmem, in_vmem),
        scratch_shapes=[
            pltpu.VMEM((n * tok, q), BF16),
            pltpu.VMEM((width, q), BF16),
            pltpu.VMEM((tok, width), BF16),
            pltpu.VMEM((count * rank, width), BF16),
            pltpu.VMEM((count * rank, q), BF16),
            pltpu.VMEM((n * tok, width), BF16),
            pltpu.VMEM((n, tok, width), BF16),
            pltpu.VMEM((tok, width), F32),
            pltpu.VMEM((n, rank, tok), BF16),
            pltpu.VMEM((n, rank, tok), BF16),
            pltpu.VMEM((rank, tok), BF16),
            pltpu.VMEM((n, rank, tok), BF16),
            pltpu.VMEM((rank + 16, tok), BF16),
            pltpu.VMEM((count * rank, tok), BF16),
            pltpu.VMEM((n, rank, width), BF16),
            pltpu.VMEM((n, rank, width), BF16),
            dma((4,)),
            dma((nc,)),
            dma((2, n, nc)),
            dma((n, nc)),
            dma((n, nc)),
            dma((n, nc)),
            dma((n,)),
            dma((n,)),
            dma,
            dma((n,)),
            dma((n,)),
            dma,
            dma((n,)),
            dma((n,)),
        ],
        compiler_params=pltpu.CompilerParams(
            collective_id=0, has_side_effects=True, vmem_limit_bytes=56 * 1024 * 1024
        ),
        cost_estimate=pl.CostEstimate(
            flops=2 * n * tok * q * width, bytes_accessed=2 * width * q, transcendentals=0
        ),
    )(dy, x, hidden, w, down.reshape(count * rank, width), up.reshape(count * rank, q), ads, live)
    return out, dgrad[None], ugrad[None]


def solution(mesh):
    n = mesh.shape["gx"]
    assert mesh.shape["gy"] == n
    placed = (
        P(("grp", "gx"), "gy"),
        P(("grp", "gy"), "gx"),
        P(("grp", "gx"), None),
        P("gx", "gy"),
        P("grp", None, "gx"),
        P("grp", None, "gy"),
        P(("grp", "gx"), None),
        P(("grp", "gx")),
    )
    return jax.shard_map(
        functools.partial(per_device, n),
        mesh=mesh,
        in_specs=placed,
        out_specs=(
            P(("grp", "gy"), "gx"),
            P(("grp", "gy"), None, "gx"),
            P(("grp", "gx"), None, "gy"),
        ),
        check_vma=False,
    )
```

time: 208 us -> 113 us (0.54)
  Pallas kernels: 0 us -> 105 us
  waiting for transfers between devices: 103 us -> 0 us
  blocking collectives: 45.8 us -> 0 us
  matrix products: 32.4 us -> 0 us
  between operations: 14.5 us -> 0.66 us
  other arithmetic: 2.99 us -> 0 us
  local copies, waits for them, and re-layouts: 9 us -> 6.86 us
    pallas_call x0 -> x1, Pallas kernels: none -> 105 us  [per_device(): pl.pallas_call(functools.partial(kernel, n), out_shape=(jax.ShapeDtypeStr...]
    all_gather x2 -> x0, waiting for transfers between devices: 102 us -> none  [the longest x1 102 us: per_device(): lax.all_gather(output_gradient, 'gx', axis=0, tiled=True)]
    dot_general x5 -> x0, matrix products: 32.4 us -> none  [the longest x1 16.6 us: contract_last(): lax.dot_general(left_side, right_side, (((1,), (1,)), ((), ())), preferre...]
    all_gather x2 -> x0, blocking collectives: 27.4 us -> none  [the longest x1 14.1 us: per_device(): every_hidden = lax.all_gather(adapter_hidden, 'gx', axis=0, tiled=True)]
    psum x1 -> x0, blocking collectives: 11.9 us -> none  [per_device(): lax.psum(partial_proj.astype(jnp.bfloat16), 'gy').astype(jnp.float32)]
    unnamed x1 -> x0, blocking collectives: 6.46 us -> none
    gather x2 -> x0, local copies, waits for them, and re-layouts: 6.05 us -> none  [the longest x1 3.22 us: per_device(): selected_up = jnp.take(adapter_up_factor, local_adapters, axis=0)]
    unnamed x19 -> x9, local copies, waits for them, and re-layouts: 1.58 us -> 6.86 us
  transfers between devices with their start and end apart: 3 -> 0, of which waited for: 1 -> 0; matrix products, arithmetic and copies ran while one was open for 20% -> 0% of each run, Pallas kernels for 0% -> 0%
where the time goes in v1:
time: 113 us
  Pallas kernels  105 us (93%)
  local copies, waits for them, and re-layouts  6.86 us (6%)
    pallas_call x1, Pallas kernels, per_device(): pl.pallas_call(functools.partial(kernel, n), out_shape=(jax.ShapeDtypeStr...  105 us
    unnamed x9, local copies, waits for them, and re-layouts  6.86 us

profile of v1, /device:TPU:0, one launch (start us, length us, event | category | flops | bytes accessed | tf_op | source)
XLA Modules:
  0.0 112.8 jit_solution(13371221155432592733)
XLA Ops:
  0.6 1.3 %copy.12.ads_ref = s32[16,1]{1,0:T(8,128)} copy(s32[16,1]{0,1:T(1,128)} %param.14) | data formatting | bytes 128 | tf_op args[6]
  2.0 1.5 %copy.11.hid_ref = bf16[256,64]{1,0:T(8,128)(2,1)} copy(bf16[256,64]{0,1:T(8,128)(2,1)} %param.10) | data formatting | bytes 65536 | tf_op args[2]
  3.5 105.2 %shard_map.103 = (bf16[256,2048]{1,0:T(8,128)(2,1)}, f32[64,2048]{1,0:T(8,128)}, f32[64,2560]{1,0:T(8,128)}) custom-call(bf16[256,2560]{1,0:T(8,128)(2,1)} %dy_hbm.1, bf16[256,2048]{1,0:T(8,128)(2,1)} %x_hbm.1, bf16[256,64]{1,0:T(8,128)(2,1)} %copy.11.hid_ref, bf16[2048,2560]{1,0:T(8,128)(2,1)} %w_hbm.1, bf16[256,2048]{1,0:T(8,128)(2,1)} %bitcast.7, ...), custom_call_target="tpu_custom_call" | custom-call | flops 10737418240 | bytes 10485760 | tf_op jit(solution)/shard_map/pallas_call | solution.py:344
  108.7 0.0 copy-start.1
  108.7 0.0 copy-start
  108.7 2.4 %copy.16 = bf16[256,2048]{1,0:T(8,128)(2,1)} copy(bf16[256,2048]{1,0:T(8,128)(2,1)} %get-tuple-element.12) | data formatting | bytes 2097152
  111.1 0.0 copy-done.1
  111.1 0.8 copy.17
  111.9 0.0 copy-done
  111.9 0.8 copy.18
Async XLA Ops:
  108.7 2.4 %copy-start.1 = (f32[64,2048]{1,0:T(8,128)S(1)}, f32[64,2048]{1,0:T(8,128)}, u32[]{:S(2)}) copy-start(f32[64,2048]{1,0:T(8,128)} %get-tuple-element.7) | copy-start | bytes 1572868
  108.7 3.2 %copy-start = (f32[64,2560]{1,0:T(8,128)S(1)}, f32[64,2560]{1,0:T(8,128)}, u32[]{:S(2)}) copy-start(f32[64,2560]{1,0:T(8,128)} %get-tuple-element.8) | copy-start | bytes 1966084

commit v2 on v1

--- a/solution.py
+++ b/solution.py
@@ -37,19 +37,23 @@
 def kernel(
     n,
     dy_hbm, x_hbm, hid_ref, w_hbm, down_hbm, up_hbm, ads_ref, live_ref,
-    out_ref, dgrad_ref, ugrad_ref,
+    out_hbm, dgrad_hbm, ugrad_hbm,
     dy_all, w, x, down, up, part, part_in, adapter_term,
-    hid_out, hid_in, proj_out, proj_in, mid, spread, dpart, dpart_in,
+    out_ref, dgrad_ref, ugrad_ref, hid_out, hid_in, proj_out, proj_in, mid, spread, dpart, dpart_in,
     load_sem, own_sem, z_send, z_recv, rs_send, rs_recv,
     hid_send, hid_recv, proj_send, proj_recv, mid_send, mid_recv, d_send, d_recv,
+    hid2_send, hid2_recv, store_sem,
 ):
     z = lax.axis_index("gx")
     c_me = lax.axis_index("gy")
     tok, q = dy_hbm.shape
     width = w_hbm.shape[0]
-    rank = hid_ref.shape[1]
+    rank = hid_ref.shape[0]
     nc = tok // CHUNK
+    parts = min(n, rank // 16)
+    part_rank = rank // parts
     tile_i = tile_of(width, 512)
+    nj = width // tile_i
     tile_q = tile_of(q, 640)
 
     def rows_of(b, c):
@@ -73,20 +77,56 @@
             device_id_type=MESH,
         )
 
-    def rs_copy(src, to, c):
-        return pltpu.make_async_remote_copy(
-            src_ref=part.at[rows_of(to, c)],
-            dst_ref=part_in.at[src, chunk_rows(c)],
-            send_sem=rs_send.at[to, c],
-            recv_sem=rs_recv.at[src, c],
+    def own_z_copy(direction, to, c):
+        return pltpu.make_async_remote_copy(
+            src_ref=dy_hbm.at[chunk_rows(c)],
+            dst_ref=dy_all.at[rows_of(z, c)],
+            send_sem=z_send.at[direction, z, c],
+            recv_sem=z_recv.at[z, c],
+            device_id={"gx": to},
+            device_id_type=MESH,
+        )
+
+    def cols_of(j):
+        return pl.ds(pl.multiple_of(j * tile_i, tile_i), tile_i)
+
+    def rs_copy(src, to, c, j):
+        return pltpu.make_async_remote_copy(
+            src_ref=part.at[rows_of(to, c), cols_of(j)],
+            dst_ref=part_in.at[src, chunk_rows(c), cols_of(j)],
+            send_sem=rs_send.at[to, c, j],
+            recv_sem=rs_recv.at[src, c, j],
             device_id={"gy": to},
             device_id_type=MESH,
         )
 
+    def part_of(src):
+        return pl.ds(pl.multiple_of(lax.min(src, parts - 1) * part_rank, part_rank), part_rank)
+
+    my_part = part_of(c_me)
+
+    def hid2_copy(src, to):
+        return pltpu.make_async_remote_copy(
+            src_ref=hid_in.at[:, part_of(src)],
+            dst_ref=hid_in.at[:, part_of(src)],
+            send_sem=hid2_send.at[to],
+            recv_sem=hid2_recv.at[src],
+            device_id={"gy": to},
+            device_id_type=MESH,
+        )
+
+    def out_copy(c):
+        return pltpu.make_async_copy(
+            out_ref.at[chunk_rows(c)], out_hbm.at[chunk_rows(c)], store_sem.at[c]
+        )
+
+    dgrad_copy = pltpu.make_async_copy(dgrad_ref, dgrad_hbm, store_sem.at[nc])
+    ugrad_copy = pltpu.make_async_copy(ugrad_ref, ugrad_hbm, store_sem.at[nc + 1])
+
     def hid_copy(src, to):
         return pltpu.make_async_remote_copy(
-            src_ref=hid_out.at[to],
-            dst_ref=hid_in.at[src],
+            src_ref=hid_out.at[to, my_part],
+            dst_ref=hid_in.at[src, my_part],
             send_sem=hid_send.at[to],
             recv_sem=hid_recv.at[src],
             device_id={"gx": to},
@@ -145,22 +185,24 @@
     pl.semaphore_wait(barrier, 2 * (n - 1))
 
     for c in range(nc):
+
+        @pl.when(z > 0)
+        def _():
+            own_z_copy(1, z - 1, c).start()
+
+        @pl.when(z < n - 1)
+        def _():
+            own_z_copy(0, z + 1, c).start()
+
+    for c in range(nc):
         own_copy(c).wait()
-
-        @pl.when(z > 0)
-        def _():
-            z_copy(1, z - 1, z, c).start()
-
-        @pl.when(z < n - 1)
-        def _():
-            z_copy(0, z + 1, z, c).start()
 
     block_of = lax.broadcasted_iota(jnp.int32, (1, tok), 1) // BLOCK_ROWS
     offset = lax.broadcasted_iota(jnp.int32, (1, tok), 1) % BLOCK_ROWS
     ad_row = jnp.zeros((1, tok), jnp.int32)
     live_row = jnp.zeros((1, tok), jnp.int32)
     for b in range(tok // BLOCK_ROWS):
-        ad_row = jnp.where(block_of == b, ads_ref[b, 0], ad_row)
+        ad_row = jnp.where(block_of == b, ads_ref[0, b], ad_row)
         live_row = jnp.where(block_of == b, live_ref[b], live_row)
     is_live = offset < live_row
 
@@ -175,13 +217,17 @@
     def _():
         proj_copy(c_me, z).start()
 
-    hid_t = jnp.transpose(hid_ref[...].astype(F32))
+    hid_t = hid_ref[...].astype(F32)
     for s in range(n):
         hid_out[s] = jnp.where((ad_row == s) & is_live, hid_t, 0.0).astype(BF16)
 
-        @pl.when(z != s)
+        @pl.when((z != s) & (c_me < parts))
         def _():
             hid_copy(z, s).start()
+
+    @pl.when(c_me < parts)
+    def _():
+        hid_in[z, my_part, :] = hid_out[z, my_part, :]
 
     loads[1].wait()
 
@@ -222,12 +268,19 @@
         for step in range(1, n):
             d_copy(c_me, lax.rem(c_me + step, n)).start()
 
+        @pl.when(c_me < parts)
+        def _():
+            for step in range(1, n):
+                hid_copy(lax.rem(z + step, n), lax.rem(z + 1, n)).wait_recv()
+            for step in range(1, n):
+                hid2_copy(c_me, lax.rem(c_me + step, n)).start()
+
     def body(i, carry):
         @pl.when(i == 2 * nc)
         def _():
             spread_middle()
 
-        @pl.when(i == 4 * nc)
+        @pl.when(i == 3 * nc)
         def _():
             adapter_work()
 
@@ -253,23 +306,35 @@
             rows = rows_of(b, c)
 
             def column(j, carry):
-                cols = pl.ds(pl.multiple_of(j * tile_i, tile_i), tile_i)
-                part[rows, cols] = nt(dy_all[rows, :], w[cols, :]).astype(BF16)
+                cols = cols_of(j)
+                part[rows, cols] = jnp.transpose(nt(w[cols, :], dy_all[rows, :])).astype(BF16)
+
+                @pl.when(b != c_me)
+                def _():
+                    rs_copy(c_me, b, c, j).start()
+
                 return carry
 
-            lax.fori_loop(0, width // tile_i, column, 0)
-
-            @pl.when(b != c_me)
-            def _():
-                rs_copy(c_me, b, c).start()
+            lax.fori_loop(0, nj, column, 0)
 
         return carry
 
     lax.fori_loop(0, 2 * nc * n, body, 0)
 
+    total = dpart[c_me].astype(F32)
     for step in range(1, n):
-        hid_copy(lax.rem(z + step, n), lax.rem(z + 1, n)).wait_recv()
-    hid_in[z] = hid_out[z]
+        src = lax.rem(c_me + step, n)
+        d_copy(src, lax.rem(c_me + 1, n)).wait_recv()
+        total = total + dpart_in[src].astype(F32)
+    dgrad_ref[...] = ADAPTER_SCALE * total
+    dgrad_copy.start()
+
+    for step in range(1, n):
+        src = lax.rem(c_me + step, n)
+
+        @pl.when(src < parts)
+        def _():
+            hid2_copy(src, lax.rem(c_me + 1, n)).wait_recv()
 
     def up_column(j, carry):
         cols = pl.ds(pl.multiple_of(j * tile_q, tile_q), tile_q)
@@ -280,25 +345,27 @@
         return carry
 
     lax.fori_loop(0, q // tile_q, up_column, 0)
-
-    total = dpart[c_me].astype(F32)
-    for step in range(1, n):
-        src = lax.rem(c_me + step, n)
-        d_copy(src, lax.rem(c_me + 1, n)).wait_recv()
-        total = total + dpart_in[src].astype(F32)
-    dgrad_ref[...] = ADAPTER_SCALE * total
-
-    def finish(c, carry):
+    ugrad_copy.start()
+
+    def finish(i, carry):
+        c = i // nj
+        j = i % nj
         rows = chunk_rows(c)
-        total = adapter_term[rows, :] + part[rows_of(c_me, c), :].astype(F32)
+        cols = cols_of(j)
+        total = adapter_term[rows, cols] + part[rows_of(c_me, c), cols].astype(F32)
         for step in range(1, n):
             src = lax.rem(c_me + step, n)
-            rs_copy(src, lax.rem(c_me + 1, n), c).wait_recv()
-            total = total + part_in[src, rows, :].astype(F32)
-        out_ref[rows, :] = total.astype(BF16)
+            rs_copy(src, lax.rem(c_me + 1, n), c, j).wait_recv()
+            total = total + part_in[src, rows, cols].astype(F32)
+        out_ref[rows, cols] = total.astype(BF16)
+
+        @pl.when(j == nj - 1)
+        def _():
+            out_copy(c).start()
+
         return carry
 
-    lax.fori_loop(0, nc, finish, 0)
+    lax.fori_loop(0, nc * nj, finish, 0)
 
     def drain(i, carry):
         b = i // nc
@@ -314,14 +381,19 @@
 
         @pl.when(b != c_me)
         def _():
-            rs_copy(c_me, b, c).wait_send()
+            for j in range(nj):
+                rs_copy(c_me, b, c, j).wait_send()
 
         return carry
 
     lax.fori_loop(0, n * nc, drain, 0)
     for step in range(1, n):
-        hid_copy(z, lax.rem(z + step, n)).wait_send()
         d_copy(c_me, lax.rem(c_me + step, n)).wait_send()
+
+        @pl.when(c_me < parts)
+        def _():
+            hid_copy(z, lax.rem(z + step, n)).wait_send()
+            hid2_copy(c_me, lax.rem(c_me + step, n)).wait_send()
 
         @pl.when(c_me == z)
         def _():
@@ -330,6 +402,23 @@
     @pl.when(c_me != z)
     def _():
         proj_copy(c_me, z).wait_send()
+
+    for c in range(nc):
+        out_copy(c).wait()
+    dgrad_copy.wait()
+    ugrad_copy.wait()
+
+
+def hand_over(a_hbm, b_hbm, c_hbm, a_out, b_out, c_out, sem):
+    copies = [
+        pltpu.make_async_copy(a_hbm, a_out, sem.at[0]),
+        pltpu.make_async_copy(b_hbm, b_out, sem.at[1]),
+        pltpu.make_async_copy(c_hbm, c_out, sem.at[2]),
+    ]
+    for copy in copies:
+        copy.start()
+    for copy in copies:
+        copy.wait()
 
 
 def per_device(n, dy, x, hidden, w, down, up, ads, live):
@@ -341,15 +430,17 @@
     in_vmem = pl.BlockSpec(memory_space=pltpu.VMEM)
     in_smem = pl.BlockSpec(memory_space=pltpu.SMEM)
     dma = pltpu.SemaphoreType.DMA
-    out, dgrad, ugrad = pl.pallas_call(
+    nj = width // tile_of(width, 512)
+    shapes = (
+        jax.ShapeDtypeStruct((tok, width), BF16),
+        jax.ShapeDtypeStruct((rank, width), F32),
+        jax.ShapeDtypeStruct((rank, q), F32),
+    )
+    results = pl.pallas_call(
         functools.partial(kernel, n),
-        out_shape=(
-            jax.ShapeDtypeStruct((tok, width), BF16),
-            jax.ShapeDtypeStruct((rank, width), F32),
-            jax.ShapeDtypeStruct((rank, q), F32),
-        ),
+        out_shape=shapes,
         in_specs=[any_space, any_space, in_vmem, any_space, any_space, any_space, in_smem, in_smem],
-        out_specs=(in_vmem, in_vmem, in_vmem),
+        out_specs=(any_space, any_space, any_space),
         scratch_shapes=[
             pltpu.VMEM((n * tok, q), BF16),
             pltpu.VMEM((width, q), BF16),
@@ -359,6 +450,9 @@
             pltpu.VMEM((n * tok, width), BF16),
             pltpu.VMEM((n, tok, width), BF16),
             pltpu.VMEM((tok, width), F32),
+            pltpu.VMEM((tok, width), BF16),
+            pltpu.VMEM((rank, width), F32),
+            pltpu.VMEM((rank, q), F32),
             pltpu.VMEM((n, rank, tok), BF16),
             pltpu.VMEM((n, rank, tok), BF16),
             pltpu.VMEM((rank, tok), BF16),
@@ -371,8 +465,8 @@
             dma((nc,)),
             dma((2, n, nc)),
             dma((n, nc)),
-            dma((n, nc)),
-            dma((n, nc)),
+            dma((n, nc, nj)),
+            dma((n, nc, nj)),
             dma((n,)),
             dma((n,)),
             dma,
@@ -381,6 +475,9 @@
             dma,
             dma((n,)),
             dma((n,)),
+            dma((n,)),
+            dma((n,)),
+            dma((nc + 2,)),
         ],
         compiler_params=pltpu.CompilerParams(
             collective_id=0, has_side_effects=True, vmem_limit_bytes=56 * 1024 * 1024
@@ -388,7 +485,14 @@
         cost_estimate=pl.CostEstimate(
             flops=2 * n * tok * q * width, bytes_accessed=2 * width * q, transcendentals=0
         ),
-    )(dy, x, hidden, w, down.reshape(count * rank, width), up.reshape(count * rank, q), ads, live)
+    )(dy, x, hidden.T, w, down.reshape(count * rank, width), up.reshape(count * rank, q), ads.T, live)
+    out, dgrad, ugrad = pl.pallas_call(
+        hand_over,
+        out_shape=shapes,
+        in_specs=[any_space] * 3,
+        out_specs=(any_space,) * 3,
+        scratch_shapes=[dma((3,))],
+    )(*results)
     return out, dgrad[None], ugrad[None]
 
 

time: 113 us -> 171 us (1.51)
  Pallas kernels: 105 us -> 170 us
  local copies, waits for them, and re-layouts: 6.86 us -> 0 us
    pallas_call x1 -> x2, Pallas kernels: 105 us -> 170 us  [the longest x1 101 us: per_device(): pl.pallas_call(functools.partial(kernel, n), out_shape=shapes, in_specs=[...]
    unnamed x9 -> x0, local copies, waits for them, and re-layouts: 6.86 us -> none
where the time goes in v2:
time: 171 us; the launch traced here: 170 us
  Pallas kernels  170 us (99%)
    pallas_call x1, Pallas kernels, per_device(): pl.pallas_call(functools.partial(kernel, n), out_shape=shapes, in_specs=[...  101 us
    pallas_call x1, Pallas kernels, per_device(): pl.pallas_call(hand_over, out_shape=shapes, in_specs=[any_space] * 3, out...  68.6 us

profile of v2, /device:TPU:0, one launch (start us, length us, event | category | flops | bytes accessed | tf_op | source)
XLA Modules:
  0.0 170.3 jit_solution(7295374123622064870)
XLA Ops:
  0.6 101.1 %shard_map.103 = (bf16[256,2048]{1,0:T(8,128)(2,1)}, f32[64,2048]{1,0:T(8,128)}, f32[64,2560]{1,0:T(8,128)}) custom-call(bf16[256,2560]{1,0:T(8,128)(2,1)} %dy_hbm.1, bf16[256,2048]{1,0:T(8,128)(2,1)} %x_hbm.1, bf16[64,256]{1,0:T(8,128)(2,1)} %bitcast.10, bf16[2048,2560]{1,0:T(8,128)(2,1)} %w_hbm.1, bf16[256,2048]{1,0:T(8,128)(2,1)} %bitcast.7, ...), custom_call_target="tpu_custom_call" | custom-call | flops 10737418240 | bytes 10485760 | tf_op jit(solution)/shard_map/pallas_call | solution.py:439
  101.7 68.6 %shard_map.104 = (bf16[256,2048]{1,0:T(8,128)(2,1)}, f32[64,2048]{1,0:T(8,128)}, f32[64,2560]{1,0:T(8,128)}) custom-call(bf16[256,2048]{1,0:T(8,128)(2,1)} %get-tuple-element.9.a_hbm, f32[64,2048]{1,0:T(8,128)} %get-tuple-element.10.b_hbm, f32[64,2560]{1,0:T(8,128)} %get-tuple-element.11.c_hbm), custom_call_target="tpu_custom_call" | custom-call | tf_op jit(solution)/shard_map/pallas_call | solution.py:489

commit v3 on v2

--- a/solution.py
+++ b/solution.py
@@ -409,15 +409,20 @@
     ugrad_copy.wait()
 
 
-def hand_over(a_hbm, b_hbm, c_hbm, a_out, b_out, c_out, sem):
-    copies = [
-        pltpu.make_async_copy(a_hbm, a_out, sem.at[0]),
-        pltpu.make_async_copy(b_hbm, b_out, sem.at[1]),
-        pltpu.make_async_copy(c_hbm, c_out, sem.at[2]),
-    ]
-    for copy in copies:
+def hand_over(a_hbm, b_hbm, c_hbm, a_out, b_out, c_out, a, b, c, in_sem, out_sem):
+    pieces = []
+    for source, held, target in ((a_hbm, a, a_out), (b_hbm, b, b_out), (c_hbm, c, c_out)):
+        half = source.shape[0] // 2
+        for start in (0, half):
+            pieces.append((source.at[start:start + half], held.at[start:start + half], target.at[start:start + half]))
+    arrive = [pltpu.make_async_copy(p[0], p[1], in_sem.at[k]) for k, p in enumerate(pieces)]
+    leave = [pltpu.make_async_copy(p[1], p[2], out_sem.at[k]) for k, p in enumerate(pieces)]
+    for copy in arrive:
         copy.start()
-    for copy in copies:
+    for k in range(len(pieces)):
+        arrive[k].wait()
+        leave[k].start()
+    for copy in leave:
         copy.wait()
 
 
@@ -491,7 +496,7 @@
         out_shape=shapes,
         in_specs=[any_space] * 3,
         out_specs=(any_space,) * 3,
-        scratch_shapes=[dma((3,))],
+        scratch_shapes=[pltpu.VMEM(t.shape, t.dtype) for t in shapes] + [dma((6,)), dma((6,))],
     )(*results)
     return out, dgrad[None], ugrad[None]
 

time: 171 us -> 104 us (0.61)
  Pallas kernels: 170 us -> 104 us
    pallas_call x1, Pallas kernels: 68.6 us -> 2.5 us  [per_device(): pl.pallas_call(hand_over, out_shape=shapes, in_specs=[any_space] * 3, out...]
where the time goes in v3:
time: 104 us
  Pallas kernels  104 us (100%)
    pallas_call x1, Pallas kernels, per_device(): pl.pallas_call(functools.partial(kernel, n), out_shape=shapes, in_specs=[...  101 us
    pallas_call x1, Pallas kernels, per_device(): pl.pallas_call(hand_over, out_shape=shapes, in_specs=[any_space] * 3, out...  2.5 us

profile of v3, /device:TPU:0, one launch (start us, length us, event | category | flops | bytes accessed | tf_op | source)
XLA Modules:
  0.0 104.2 jit_solution(12655470319911530849)
XLA Ops:
  0.6 101.1 %shard_map.103 = (bf16[256,2048]{1,0:T(8,128)(2,1)}, f32[64,2048]{1,0:T(8,128)}, f32[64,2560]{1,0:T(8,128)}) custom-call(bf16[256,2560]{1,0:T(8,128)(2,1)} %dy_hbm.1, bf16[256,2048]{1,0:T(8,128)(2,1)} %x_hbm.1, bf16[64,256]{1,0:T(8,128)(2,1)} %bitcast.10, bf16[2048,2560]{1,0:T(8,128)(2,1)} %w_hbm.1, bf16[256,2048]{1,0:T(8,128)(2,1)} %bitcast.7, ...), custom_call_target="tpu_custom_call" | custom-call | flops 10737418240 | bytes 10485760 | tf_op jit(solution)/shard_map/pallas_call | solution.py:444
  101.7 2.5 %shard_map.104 = (bf16[256,2048]{1,0:T(8,128)(2,1)}, f32[64,2048]{1,0:T(8,128)}, f32[64,2560]{1,0:T(8,128)}) custom-call(bf16[256,2048]{1,0:T(8,128)(2,1)} %get-tuple-element.9.a_hbm, f32[64,2048]{1,0:T(8,128)} %get-tuple-element.10.b_hbm, f32[64,2560]{1,0:T(8,128)} %get-tuple-element.11.c_hbm), custom_call_target="tpu_custom_call" | custom-call | tf_op jit(solution)/shard_map/pallas_call | solution.py:494

commit v4 on v3

--- a/solution.py
+++ b/solution.py
@@ -52,7 +52,7 @@
     nc = tok // CHUNK
     parts = min(n, rank // 16)
     part_rank = rank // parts
-    tile_i = tile_of(width, 512)
+    tile_i = tile_of(width, 256)
     nj = width // tile_i
     tile_q = tile_of(q, 640)
 
@@ -412,9 +412,9 @@
 def hand_over(a_hbm, b_hbm, c_hbm, a_out, b_out, c_out, a, b, c, in_sem, out_sem):
     pieces = []
     for source, held, target in ((a_hbm, a, a_out), (b_hbm, b, b_out), (c_hbm, c, c_out)):
-        half = source.shape[0] // 2
-        for start in (0, half):
-            pieces.append((source.at[start:start + half], held.at[start:start + half], target.at[start:start + half]))
+        quarter = source.shape[0] // 4
+        for start in range(0, source.shape[0], quarter):
+            pieces.append((source.at[start:start + quarter], held.at[start:start + quarter], target.at[start:start + quarter]))
     arrive = [pltpu.make_async_copy(p[0], p[1], in_sem.at[k]) for k, p in enumerate(pieces)]
     leave = [pltpu.make_async_copy(p[1], p[2], out_sem.at[k]) for k, p in enumerate(pieces)]
     for copy in arrive:
@@ -435,7 +435,7 @@
     in_vmem = pl.BlockSpec(memory_space=pltpu.VMEM)
     in_smem = pl.BlockSpec(memory_space=pltpu.SMEM)
     dma = pltpu.SemaphoreType.DMA
-    nj = width // tile_of(width, 512)
+    nj = width // tile_of(width, 256)
     shapes = (
         jax.ShapeDtypeStruct((tok, width), BF16),
         jax.ShapeDtypeStruct((rank, width), F32),
@@ -496,7 +496,7 @@
         out_shape=shapes,
         in_specs=[any_space] * 3,
         out_specs=(any_space,) * 3,
-        scratch_shapes=[pltpu.VMEM(t.shape, t.dtype) for t in shapes] + [dma((6,)), dma((6,))],
+        scratch_shapes=[pltpu.VMEM(t.shape, t.dtype) for t in shapes] + [dma((12,)), dma((12,))],
     )(*results)
     return out, dgrad[None], ugrad[None]
 

time: 104 us -> 112 us (1.077)
  Pallas kernels: 104 us -> 111 us
    pallas_call x1, Pallas kernels: 101 us -> 108 us  [per_device(): pl.pallas_call(functools.partial(kernel, n), out_shape=shapes, in_specs=[...]
where the time goes in v4:
time: 112 us; the launch traced here: 111 us
  Pallas kernels  111 us (99%)
    pallas_call x1, Pallas kernels, per_device(): pl.pallas_call(functools.partial(kernel, n), out_shape=shapes, in_specs=[...  108 us
    pallas_call x1, Pallas kernels, per_device(): pl.pallas_call(hand_over, out_shape=shapes, in_specs=[any_space] * 3, out...  2.51 us

profile of v4, /device:TPU:0, one launch (start us, length us, event | category | flops | bytes accessed | tf_op | source)
XLA Modules:
  0.0 111.5 jit_solution(3823583858329875136)
XLA Ops:
  0.6 108.3 %shard_map.103 = (bf16[256,2048]{1,0:T(8,128)(2,1)}, f32[64,2048]{1,0:T(8,128)}, f32[64,2560]{1,0:T(8,128)}) custom-call(bf16[256,2560]{1,0:T(8,128)(2,1)} %dy_hbm.1, bf16[256,2048]{1,0:T(8,128)(2,1)} %x_hbm.1, bf16[64,256]{1,0:T(8,128)(2,1)} %bitcast.10, bf16[2048,2560]{1,0:T(8,128)(2,1)} %w_hbm.1, bf16[256,2048]{1,0:T(8,128)(2,1)} %bitcast.7, ...), custom_call_target="tpu_custom_call" | custom-call | flops 10737418240 | bytes 10485760 | tf_op jit(solution)/shard_map/pallas_call | solution.py:444
  109.0 2.5 %shard_map.104 = (bf16[256,2048]{1,0:T(8,128)(2,1)}, f32[64,2048]{1,0:T(8,128)}, f32[64,2560]{1,0:T(8,128)}) custom-call(bf16[256,2048]{1,0:T(8,128)(2,1)} %get-tuple-element.9.a_hbm, f32[64,2048]{1,0:T(8,128)} %get-tuple-element.10.b_hbm, f32[64,2560]{1,0:T(8,128)} %get-tuple-element.11.c_hbm), custom_call_target="tpu_custom_call" | custom-call | tf_op jit(solution)/shard_map/pallas_call | solution.py:494
